TPU v7x, 32 devices: a whole 2x2x4 slice. The times are simulated.
32 devices in a mesh: lat: 4 (over x, core), lon: 8 (over z, y).
Axes of the slice: x: 2, y: 2, z: 4, core: 2. Of those that a mesh axis runs over, the one named last changes fastest.
Arguments:
- control: float32 [16, 256, 8192], P(None, 'lat', 'lon'), may hold values from -6 to 6
- sigma_field: float32 [16, 256, 8192], P(None, 'lat', 'lon'), may hold values from 0.3 to 3
- mixing: float32 [16, 16], replicated, may hold values from -1.5 to 1.5
- zonal_reach: int32 [256], P('lat'), may hold values from 1 to 64, as said below
- obs_owner: int32 [65536, 1], P(('lat', 'lon')), may hold values from 0 to 31; in each aligned block of 2048 rows (0 to 2047, 2048 to 4095, ...) at most 64 rows name the same one
- obs_cell: int32 [65536], P(('lat', 'lon')), may hold values from 0 to 65535
- obs_chan: int32 [65536], P(('lat', 'lon')), may hold values from 0 to 15
- obs_weight: bfloat16 [65536], P(('lat', 'lon')), may hold values from -48 to 48
Outputs:
- increment: float32 [16, 256, 8192], P(None, 'lat', 'lon')
- gradient: float32 [16, 256, 8192], P(None, 'lat', 'lon')
Inputs may be any that keep to these rules, and one draw needn't show every extreme that they name: `zonal_reach`: rows next to either pole have reach 64. `obs_owner`: devices are numbered in the order of the joined axis lat+lon; among the observations held by one device at most 64 name the same owner.
All inputs are finite; a program needn't handle non-finite values.
Results may differ from a plain program's by a relative error of at most 0.0003.
Values may be sent and summed in bfloat16 or wider, within the bound.
A program may use at most 128 MiB of HBM per device.

v0:
```python
import math

import jax
import jax.numpy as jnp
from jax import lax
from jax.experimental import pallas as pl
from jax.experimental.pallas import tpu as pltpu
from jax.sharding import PartitionSpec as P

CAP = 64
MAXREACH = 64
MREACH = 8
GROUP = 16
TILE = 128
BF = jnp.bfloat16
F32 = jnp.float32
LOG2E = math.log2(math.e)


def merid_weights(lag):
    taps = [math.exp(-0.5 * (3.0 * t / MREACH) ** 2) for t in range(-MREACH, MREACH + 1)]
    norm = math.sqrt(sum(w * w for w in taps))
    scaled = lag * (3.0 / MREACH)
    return jnp.where(jnp.abs(lag) <= MREACH, jnp.exp(-0.5 * scaled * scaled) / norm, 0.0)


def kron_matrices(mixing):
    channels = mixing.shape[0]
    a = jnp.arange(GROUP)[:, None]
    p = jnp.arange(2 * GROUP)[None, :]
    band = merid_weights((p - a - MREACH).astype(F32)).reshape(GROUP, 2, GROUP)
    size = GROUP * channels
    fwd = band.transpose(1, 0, 2)[:, :, None, None, :] * mixing[None, None, :, :, None]
    fwd = fwd.reshape(2, size, size)
    adj = band.transpose(1, 0, 2)[:, None, :, :, None] * mixing.T[None, :, None, None, :]
    adj = adj.reshape(2, size, size)
    return fwd, adj


def row_params(zonal_reach):
    reach = zonal_reach.astype(F32)
    t = jnp.arange(-MAXREACH, MAXREACH + 1).astype(F32)
    scaled = 3.0 * t[None, :] / reach[:, None]
    taps = jnp.where(jnp.abs(t)[None, :] <= reach[:, None], jnp.exp(-0.5 * scaled * scaled), 0.0)
    log_norm = -0.5 * jnp.log2(jnp.sum(taps * taps, axis=1))
    return jnp.stack([-4.5 * LOG2E / (reach * reach), log_norm, reach * reach])


def split(x):
    hi = x.astype(BF)
    return hi, (x - hi.astype(F32)).astype(BF)


def dot(a, b):
    return jnp.dot(a, b, preferred_element_type=F32)


def lag_squared():
    p = lax.broadcasted_iota(jnp.int32, (2 * TILE, TILE), 0)
    j = lax.broadcasted_iota(jnp.int32, (2 * TILE, TILE), 1)
    lag = (p - j - MAXREACH).astype(F32)
    return lag * lag


def zonal_rows(hi_ref, lo_ref, out_ref, params_ref, first_row, blocks):
    t2 = lag_squared()
    channels = hi_ref.shape[0] // GROUP
    for r in range(GROUP):
        row = first_row + r
        coef, shift, limit = params_ref[0, row], params_ref[1, row], params_ref[2, row]
        band = jnp.where(t2 <= limit, jnp.exp2(t2 * coef + shift), 0.0)
        band = jnp.concatenate(split(band), axis=1)
        rows = slice(r * channels, (r + 1) * channels)
        parts = []
        for ref in (hi_ref, lo_ref):
            for b in range(blocks):
                parts.append(ref[rows, b * TILE:(b + 2) * TILE])
        prod = dot(jnp.concatenate(parts, axis=0), band)
        n = blocks * channels
        total = prod[:n, :TILE] + (prod[:n, TILE:] + prod[n:, :TILE])
        for b in range(blocks):
            out_ref[rows, b * TILE:(b + 1) * TILE] = total[b * channels:(b + 1) * channels]


def prep_kernel(devices, owner_ref, cell_ref, chan_ref, weight_ref, out_ref):
    count = owner_ref.shape[1]
    chunk = math.gcd(count, 256)
    owner = owner_ref[...]
    hits = lax.broadcasted_iota(jnp.int32, (devices, count), 0) == owner
    hits_f = jnp.where(hits, 1.0, 0.0)
    hits_b = hits_f.astype(BF)
    upper = (
        lax.broadcasted_iota(jnp.int32, (chunk, chunk), 0)
        < lax.broadcasted_iota(jnp.int32, (chunk, chunk), 1)
    )
    upper = jnp.where(upper, 1.0, 0.0).astype(BF)
    base = jnp.zeros((devices, 1), F32)
    ranks = []
    for k in range(count // chunk):
        cols = slice(k * chunk, (k + 1) * chunk)
        before = dot(hits_b[:, cols], upper) + base
        ranks.append(jnp.sum(before * hits_f[:, cols], axis=0, keepdims=True))
        base = base + jnp.sum(hits_f[:, cols], axis=1, keepdims=True)
    rank = jnp.concatenate(ranks, axis=1).astype(jnp.int32)
    rank_hits = lax.broadcasted_iota(jnp.int32, (CAP, count), 0) == rank
    flat = cell_ref[...] + chan_ref[...]
    digits = [flat & 127, (flat >> 7) & 127, flat >> 14]
    pieces = [weight_ref[...].astype(F32)] + [d.astype(F32) for d in digits]
    table = jnp.concatenate([jnp.where(rank_hits, v, 0.0) for v in pieces], axis=0).astype(BF)
    out = lax.dot_general(hits_b, table, (((1,), (1,)), ((), ())), preferred_element_type=F32)
    out_ref[...] = out.astype(BF)


def adjoint_kernel(
    params_ref, got_ref, sigma_ref, kron_ref, out_ref,
    colhot, work, hi_ref, lo_ref, zon_ref, carry, kron_hi, kron_lo,
):
    step = pl.program_id(0)
    groups = pl.num_programs(0) - 1
    channels, _, cols = sigma_ref.shape
    received = got_ref.shape[1]
    lines = channels * GROUP
    wide = cols + TILE
    chunk = math.gcd(received, 2048)

    def place(k):
        digits = got_ref[:, k * chunk:(k + 1) * chunk].astype(F32)
        flat = digits[1:2] + 128.0 * digits[2:3] + 16384.0 * digits[3:4]
        return digits[0:1], flat.astype(jnp.int32)

    @pl.when(step == 0)
    def _():
        hi, lo = split(kron_ref[...])
        kron_hi[...] = hi
        kron_lo[...] = lo
        carry[...] = jnp.zeros_like(carry)
        hi_ref[...] = jnp.zeros_like(hi_ref)
        lo_ref[...] = jnp.zeros_like(lo_ref)
        for k in range(received // chunk):
            col = place(k)[1] % cols
            hot = lax.broadcasted_iota(jnp.int32, (cols, chunk), 0) == col
            colhot[:, k * chunk:(k + 1) * chunk] = jnp.where(hot, 1.0, 0.0).astype(BF)

    @pl.when(step < groups)
    def _():
        place_ids = lax.broadcasted_iota(jnp.int32, (lines, chunk), 0)
        total = jnp.zeros((lines, cols), F32)
        for k in range(received // chunk):
            value, flat = place(k)
            line = flat // cols
            chan, row = line % channels, line // channels - step * GROUP
            inside = (row >= 0) & (row < GROUP)
            target = jnp.where(inside, chan * GROUP + row, -1)
            rowhot = jnp.where(place_ids == target, value, 0.0).astype(BF)
            total = total + lax.dot_general(
                rowhot, colhot[:, k * chunk:(k + 1) * chunk],
                (((1,), (1,)), ((), ())), preferred_element_type=F32,
            )
        weighted = total.reshape(channels, GROUP, cols) * sigma_ref[...]
        weighted = jnp.swapaxes(weighted, 0, 1).reshape(lines, cols)
        hi, lo = split(weighted)
        hi_ref[:, TILE:TILE + cols] = hi
        lo_ref[:, TILE:TILE + cols] = lo
        zonal_rows(hi_ref, lo_ref, zon_ref, params_ref, step * GROUP, wide // TILE)
        z_hi, z_lo = split(zon_ref[...])
        done = carry[...] + (
            dot(kron_hi[1], z_hi) + (dot(kron_hi[1], z_lo) + dot(kron_lo[1], z_hi))
        )
        out_ref[...] = done.reshape(channels, GROUP, wide)
        carry[...] = dot(kron_hi[0], z_hi) + (dot(kron_hi[0], z_lo) + dot(kron_lo[0], z_hi))

    @pl.when(step == groups)
    def _():
        out_ref[...] = carry[...].reshape(channels, GROUP, wide)


def forward_kernel(
    params_ref, low_ref, high_ref, sigma_ref, kron_ref, out_ref,
    hi_ref, lo_ref, zon_ref, kron_hi, kron_lo,
):
    step = pl.program_id(0)
    channels, _, cols = sigma_ref.shape
    lines = channels * GROUP
    wide = cols + TILE

    @pl.when(step == 0)
    def _():
        hi, lo = split(kron_ref[...])
        kron_hi[...] = hi
        kron_lo[...] = lo

    total = None
    for half, ref in enumerate((low_ref, high_ref)):
        hi, lo = split(ref[...].reshape(lines, wide))
        part = dot(kron_hi[half], hi) + (dot(kron_hi[half], lo) + dot(kron_lo[half], hi))
        total = part if total is None else total + part
    hi, lo = split(total)
    hi_ref[...] = hi
    lo_ref[...] = lo
    zonal_rows(hi_ref, lo_ref, zon_ref, params_ref, step * GROUP, cols // TILE)
    smooth = jnp.swapaxes(zon_ref[...].reshape(GROUP, channels, cols), 0, 1)
    out_ref[...] = smooth * sigma_ref[...]


def shifts(axis, periodic):
    count = lax.axis_size(axis)
    forward = [(i, i + 1) for i in range(count - 1)]
    if periodic:
        forward.append((count - 1, 0))
    return forward, [(t, s) for s, t in forward]


def local(control, sigma_field, mixing, zonal_reach, obs_owner, obs_cell, obs_chan, obs_weight):
    channels, rows, cols = control.shape
    devices = lax.axis_size("lat") * lax.axis_size("lon")
    lines, wide, groups = channels * GROUP, cols + TILE, rows // GROUP
    lat_fwd, lat_bwd = shifts("lat", False)
    lon_fwd, lon_bwd = shifts("lon", True)

    low = lax.ppermute(control[:, rows - MREACH:, :], "lat", lat_fwd)
    high = lax.ppermute(control[:, :MREACH, :], "lat", lat_bwd)

    count = obs_cell.shape[0]
    owner = obs_owner.reshape(1, count)
    row, col = obs_cell // cols, obs_cell % cols
    sent = pl.pallas_call(
        lambda *refs: prep_kernel(devices, *refs),
        out_shape=jax.ShapeDtypeStruct((devices, 4 * CAP), BF),
        compiler_params=pltpu.CompilerParams(vmem_limit_bytes=48 * 2**20),
        name="prep",
    )(
        owner,
        (row * (channels * cols) + col).reshape(1, count),
        (obs_chan * cols).reshape(1, count),
        obs_weight.reshape(1, count),
    )
    got = lax.all_to_all(sent, ("lat", "lon"), split_axis=0, concat_axis=0, tiled=True)
    received = devices * CAP
    got = got.reshape(devices, 4, CAP).transpose(1, 0, 2).reshape(4, received)

    params = row_params(zonal_reach)
    kron_fwd, kron_adj = kron_matrices(mixing)

    tall = jnp.concatenate([low, control, high], axis=1)
    left = lax.ppermute(tall[:, :, cols - MAXREACH:], "lon", lon_fwd)
    right = lax.ppermute(tall[:, :, :MAXREACH], "lon", lon_bwd)
    padded = jnp.concatenate([left, tall, right], axis=2)

    smem = pl.BlockSpec(memory_space=pltpu.SMEM)
    vmem = pl.BlockSpec(memory_space=pltpu.VMEM)
    ext = pl.pallas_call(
        adjoint_kernel,
        grid=(groups + 1,),
        in_specs=[
            smem,
            vmem,
            pl.BlockSpec((channels, GROUP, cols), lambda g: (0, jnp.minimum(g, groups - 1), 0)),
            vmem,
        ],
        out_specs=pl.BlockSpec((channels, GROUP, wide), lambda g: (0, g, 0)),
        out_shape=jax.ShapeDtypeStruct((channels, rows + GROUP, wide), F32),
        scratch_shapes=[
            pltpu.VMEM((cols, received), BF),
            pltpu.VMEM((lines, cols), F32),
            pltpu.VMEM((lines, wide + TILE), BF),
            pltpu.VMEM((lines, wide + TILE), BF),
            pltpu.VMEM((lines, wide), F32),
            pltpu.VMEM((lines, wide), F32),
            pltpu.VMEM((2, lines, lines), BF),
            pltpu.VMEM((2, lines, lines), BF),
        ],
        compiler_params=pltpu.CompilerParams(vmem_limit_bytes=52 * 2**20),
        cost_estimate=pl.CostEstimate(
            flops=16 * 10**9, bytes_accessed=10 * 2**20, transcendentals=0
        ),
        name="adjoint",
    )(params, got, sigma_field, kron_adj)

    to_left = lax.ppermute(ext[:, :, :MAXREACH], "lon", lon_bwd)
    to_right = lax.ppermute(ext[:, :, cols + MAXREACH:], "lon", lon_fwd)

    increment = pl.pallas_call(
        forward_kernel,
        grid=(groups,),
        in_specs=[
            smem,
            pl.BlockSpec((channels, GROUP, wide), lambda g: (0, g, 0)),
            pl.BlockSpec((channels, GROUP, wide), lambda g: (0, g + 1, 0)),
            pl.BlockSpec((channels, GROUP, cols), lambda g: (0, g, 0)),
            vmem,
        ],
        out_specs=pl.BlockSpec((channels, GROUP, cols), lambda g: (0, g, 0)),
        out_shape=jax.ShapeDtypeStruct((channels, rows, cols), F32),
        scratch_shapes=[
            pltpu.VMEM((lines, wide), BF),
            pltpu.VMEM((lines, wide), BF),
            pltpu.VMEM((lines, cols), F32),
            pltpu.VMEM((2, lines, lines), BF),
            pltpu.VMEM((2, lines, lines), BF),
        ],
        compiler_params=pltpu.CompilerParams(vmem_limit_bytes=48 * 2**20),
        cost_estimate=pl.CostEstimate(
            flops=12 * 10**9, bytes_accessed=20 * 2**20, transcendentals=0
        ),
        name="forward",
    )(params, padded, padded, sigma_field, kron_fwd)

    inner = ext[:, :, MAXREACH:MAXREACH + cols]
    inner = inner + jnp.pad(to_right, ((0, 0), (0, 0), (0, cols - MAXREACH)))
    inner = inner + jnp.pad(to_left, ((0, 0), (0, 0), (cols - MAXREACH, 0)))
    to_up = lax.ppermute(inner[:, :MREACH], "lat", lat_bwd)
    to_down = lax.ppermute(inner[:, rows + MREACH:], "lat", lat_fwd)
    gradient = inner[:, MREACH:MREACH + rows]
    gradient = gradient + jnp.pad(to_down, ((0, 0), (0, rows - MREACH), (0, 0)))
    gradient = gradient + jnp.pad(to_up, ((0, 0), (rows - MREACH, 0), (0, 0)))
    return (increment, gradient)


def solution(mesh):
    return jax.shard_map(
        local,
        mesh=mesh,
        in_specs=(
            P(None, "lat", "lon"),
            P(None, "lat", "lon"),
            P(),
            P("lat"),
            P(("lat", "lon"), None),
            P(("lat", "lon")),
            P(("lat", "lon")),
            P(("lat", "lon")),
        ),
        out_specs=(P(None, "lat", "lon"), P(None, "lat", "lon")),
        check_vma=False,
    )
```

profile of v0, /device:TPU:1, one launch (start us, length us, event | category | flops | bytes accessed | tf_op | source)
XLA Modules:
  0.0 138.6 jit_solution(9382186606125699641)
XLA Ops:
  5.9 7.1 %all-to-all-start = ((bf16[32,2,128]{2,1,0:T(2,128)(2,1)}), bf16[32,2,128]{2,1,0:T(2,128)(2,1)S(1)}, u32[]{:S(2)}, u32[]{:S(2)}) async-start(bf16[32,2,128]{2,1,0:T(2,128)(2,1)} %reshape.79), calls=%async_computation | async-start | bytes 32768 | tf_op jit(solution)/shard_map/all_to_all | solution.py:237
  13.0 2.3 %fusion.15 = (f32[16,8,1024]{2,1,0:T(8,128)}, f32[16,8,1024]{2,1,0:T(8,128)}) fusion(f32[16,64,1024]{2,1,0:T(8,128)} %param.8), kind=kLoop, calls=%fused_computation.40 | loop fusion | bytes 2097152 | tf_op jit(solution)/shard_map/slice | solution.py:221
  15.3 3.5 %collective-permute-start = (f32[16,8,1024]{2,1,0:T(8,128)}, f32[16,8,1024]{2,1,0:T(8,128)S(1)}, u32[]{:S(2)}, u32[]{:S(2)}) collective-permute-start(f32[16,8,1024]{2,1,0:T(8,128)} %get-tuple-element.9), channel_id=1, source_target_pairs={{0,8},{8,16},{16,24},{1,9},{9,17},{17,25},{2,10},{10,18},{18,26},{... | collective-permute-start | bytes 1572872 | tf_op jit(solution)/shard_map/ppermute | solution.py:220
  22.3 2.5 %mul.144 = f32[2,16,16,16,16]{4,3,2,1,0:T(8,128)} broadcast(f32[2,16,16]{2,1,0:T(8,128)S(1)} %multiply_select_fusion), dimensions={0,2,3} | broadcast | bytes 526336 | tf_op jit(solution)/shard_map/mul | solution.py:35
  24.9 3.5 %mul.145 = f32[2,256,256]{2,1,0:T(8,128)S(1)} reshape(f32[2,16,16,16,16]{4,3,2,1,0:T(8,128)} %mul.144) | data formatting | bytes 1048576 | tf_op jit(solution)/shard_map/mul | solution.py:35
  28.8 18.3 %adjoint.1 = f32[16,80,1152]{2,1,0:T(8,128)} custom-call(f32[3,64]{1,0:T(4,128)S(1)} %pad_maximum_fusion.params_ref, bf16[4,2048]{1,0:T(4,128)(2,1)S(1)} %reshape.77.got_ref, f32[16,64,1024]{2,1,0:T(8,128)} %sigma_ref.3, f32[2,256,256]{2,1,0:T(8,128)S(1)} %broadcast_multiply_fusion.kron_ref), custom_call_target="tpu_custom_call" | custom-call | flops 16000000000 | bytes 10485760 | tf_op jit(solution)/shard_map/adjoint/pallas_call | solution.py:251
  49.6 4.0 %collective-permute-start.5 = (f32[16,80,64]{1,2,0:T(8,128)}, f32[16,80,64]{1,2,0:T(8,128)}, u32[]{:S(2)}, u32[]{:S(2)}) collective-permute-start(f32[16,80,64]{1,2,0:T(8,128)} %copy.43), channel_id=1, source_target_pairs={{1,0},{2,1},{3,2},{4,3},{5,4},{6,5},{7,6},{0,7},{9,8},{10,9},{11,1... | collective-permute-start | bytes 983048 | tf_op jit(solution)/shard_map/ppermute | solution.py:279
  54.7 2.1 %collective-permute-start.1 = (f32[16,8,1024]{2,1,0:T(8,128)}, f32[16,8,1024]{2,1,0:T(8,128)}, u32[]{:S(2)}, u32[]{:S(2)}) collective-permute-start(f32[16,8,1024]{2,1,0:T(8,128)} %get-tuple-element.8), channel_id=1, source_target_pairs={{8,0},{16,8},{24,16},{9,1},{17,9},{25,17},{10,2},{18,10},{26,18},{... | collective-permute-start | bytes 1572872 | tf_op jit(solution)/shard_map/ppermute | solution.py:221
  58.0 2.3 %mul.135 = f32[2,16,16,16,16]{4,3,2,1,0:T(8,128)} broadcast(f32[2,16,16]{2,1,0:T(8,128)S(1)} %multiply_select_fusion), dimensions={0,1,4} | broadcast | bytes 526336 | tf_op jit(solution)/shard_map/mul | solution.py:33
  60.3 3.5 %mul.136 = f32[2,256,256]{2,1,0:T(8,128)S(1)} reshape(f32[2,16,16,16,16]{4,3,2,1,0:T(8,128)} %mul.135) | data formatting | bytes 1048576 | tf_op jit(solution)/shard_map/mul | solution.py:33
  63.9 10.3 %collective-permute-done.5 = f32[16,80,64]{1,2,0:T(8,128)} collective-permute-done((f32[16,80,64]{1,2,0:T(8,128)}, f32[16,80,64]{1,2,0:T(8,128)}, u32[]{:S(2)}, u32[]{:S(2)}) %collective-permute-start.5) | collective-permute-done | bytes 327712 | tf_op jit(solution)/shard_map/ppermute | solution.py:279
  76.8 2.5 %constant_dynamic-update-slice_fusion.1 = f32[16,80,1024]{2,1,0:T(8,128)S(1)} fusion(f32[16,80,1024]{2,1,0:T(8,128)S(1)} %constant_dynamic-update-slice_fusion.2, f32[16,64,1024]{2,1,0:T(8,128)} %param.8), kind=kLoop, calls=%fused_computation.21 | loop fusion | bytes 8388608
  80.4 2.4 %copy-done.3 = f32[16,80,1024]{2,1,0:T(8,128)} copy-done((f32[16,80,1024]{2,1,0:T(8,128)}, f32[16,80,1024]{2,1,0:T(8,128)S(1)}, u32[]{:S(2)}) %copy-start.3) | copy-done | bytes 5242904
  86.3 3.4 %collective-permute-start.3 = (f32[16,80,64]{1,2,0:T(8,128)}, f32[16,80,64]{1,2,0:T(8,128)}, u32[]{:S(2)}, u32[]{:S(2)}) collective-permute-start(f32[16,80,64]{1,2,0:T(8,128)} %copy.35), channel_id=1, source_target_pairs={{1,0},{2,1},{3,2},{4,3},{5,4},{6,5},{7,6},{0,7},{9,8},{10,9},{11,1... | collective-permute-start | bytes 983048 | tf_op jit(solution)/shard_map/ppermute | solution.py:246
  89.7 4.3 %fusion = f32[16,80,1024]{2,1,0:T(8,128)S(1)} fusion(f32[16,80,1152]{2,1,0:T(8,128)} %adjoint.1, f32[16,80,64]{2,1,0:T(8,128)S(1)} %copy.44, f32[16,80,64]{2,1,0:T(8,128)S(1)} %copy.42), kind=kLoop, calls=%fused_computation.1 | loop fusion | flops 2621440 | bytes 11141120 | tf_op jit(solution)/shard_map/add | solution.py:310
  94.0 2.3 %copy-done.2 = f32[16,80,1024]{2,1,0:T(8,128)} copy-done((f32[16,80,1024]{2,1,0:T(8,128)}, f32[16,80,1024]{2,1,0:T(8,128)S(1)}, u32[]{:S(2)}) %copy-start.2) | copy-done | bytes 5242904
  97.4 2.3 %collective-permute-start.6 = (f32[16,8,1024]{2,1,0:T(8,128)}, f32[16,8,1024]{2,1,0:T(8,128)S(1)}, u32[]{:S(2)}, u32[]{:S(2)}) collective-permute-start(f32[16,8,1024]{2,1,0:T(8,128)} %get-tuple-element.4), channel_id=1, source_target_pairs={{0,8},{8,16},{16,24},{1,9},{9,17},{17,25},{2,10},{10,18},{18,26},{... | collective-permute-start | bytes 1572872 | tf_op jit(solution)/shard_map/ppermute | solution.py:312
  99.7 2.0 %collective-permute-start.7 = (f32[16,8,1024]{2,1,0:T(8,128)}, f32[16,8,1024]{2,1,0:T(8,128)}, u32[]{:S(2)}, u32[]{:S(2)}) collective-permute-start(f32[16,8,1024]{2,1,0:T(8,128)} %get-tuple-element.5), channel_id=1, source_target_pairs={{8,0},{16,8},{24,16},{9,1},{17,9},{25,17},{10,2},{18,10},{26,18},{... | collective-permute-start | bytes 1572872 | tf_op jit(solution)/shard_map/ppermute | solution.py:311
  101.7 7.1 %collective-permute-done.2 = f32[16,80,64]{1,2,0:T(8,128)S(1)} collective-permute-done((f32[16,80,64]{1,2,0:T(8,128)}, f32[16,80,64]{1,2,0:T(8,128)S(1)}, u32[]{:S(2)}, u32[]{:S(2)}) %collective-permute-start.2) | collective-permute-done | bytes 327712 | tf_op jit(solution)/shard_map/ppermute | solution.py:245
  109.0 1.6 %collective-permute-done.3 = f32[16,80,64]{1,2,0:T(8,128)} collective-permute-done((f32[16,80,64]{1,2,0:T(8,128)}, f32[16,80,64]{1,2,0:T(8,128)}, u32[]{:S(2)}, u32[]{:S(2)}) %collective-permute-start.3) | collective-permute-done | bytes 327712 | tf_op jit(solution)/shard_map/ppermute | solution.py:246
  112.0 8.2 %concatenate.7.low_ref.high_ref = f32[16,80,1152]{2,1,0:T(8,128)} concatenate(f32[16,80,64]{2,1,0:T(8,128)S(1)} %copy.36, f32[16,80,1024]{2,1,0:T(8,128)} %copy-done.3, f32[16,80,64]{2,1,0:T(8,128)S(1)} %copy.37), dimensions={2} | concatenate | bytes 11796480 | tf_op jit(solution)/shard_map/concatenate | solution.py:247
  120.2 2.2 %copy-done.1 = f32[16,64,1024]{2,1,0:T(8,128)S(1)} copy-done((f32[16,64,1024]{2,1,0:T(8,128)S(1)}, f32[16,64,1024]{2,1,0:T(8,128)}, u32[]{:S(2)}) %copy-start.1) | copy-done | bytes 4194328
  122.4 12.5 %forward.1 = f32[16,64,1024]{2,1,0:T(8,128)} custom-call(f32[3,64]{1,0:T(4,128)S(1)} %pad_maximum_fusion.params_ref, f32[16,80,1152]{2,1,0:T(8,128)} %concatenate.7.low_ref.high_ref, f32[16,80,1152]{2,1,0:T(8,128)} %concatenate.7.low_ref.high_ref, f32[16,64,1024]{2,1,0:T(8,128)S(1)} %copy-done.1, f32[2,256,256]{2,1,0:T(8,128)S(1)} %broadcast_multiply_fusion.1.kron_ref), custom_call_target="tpu_custom_call" | custom-call | flops 12000000000 | bytes 20971520 | tf_op jit(solution)/shard_map/forward/pallas_call | solution.py:282
  135.0 3.6 %fusion.1 = f32[16,64,1024]{2,1,0:T(8,128)} fusion(f32[16,80,1024]{2,1,0:T(8,128)S(1)} %bitcast.25, f32[16,8,1024]{2,1,0:T(8,128)} %collective-permute-done.7, f32[16,8,1024]{2,1,0:T(8,128)S(1)} %collective-permute-done.6), kind=kLoop, calls=%fused_computation.3 | loop fusion | flops 2097152 | bytes 9437184 | tf_op jit(solution)/shard_map/add | solution.py:315
  (60 shorter events, 23.7 us)
Async XLA Ops:
  2.7 0.7 copy-start
  5.9 22.5 %all-to-all-start = ((bf16[32,2,128]{2,1,0:T(2,128)(2,1)}), bf16[32,2,128]{2,1,0:T(2,128)(2,1)S(1)}, u32[]{:S(2)}, u32[]{:S(2)}) async-start(bf16[32,2,128]{2,1,0:T(2,128)(2,1)} %reshape.79), calls=%async_computation | async-start | bytes 32768 | tf_op jit(solution)/shard_map/all_to_all | solution.py:237
  15.3 61.4 %collective-permute-start = (f32[16,8,1024]{2,1,0:T(8,128)}, f32[16,8,1024]{2,1,0:T(8,128)S(1)}, u32[]{:S(2)}, u32[]{:S(2)}) collective-permute-start(f32[16,8,1024]{2,1,0:T(8,128)} %get-tuple-element.9), channel_id=1, source_target_pairs={{0,8},{8,16},{16,24},{1,9},{9,17},{17,25},{2,10},{10,18},{18,26},{... | collective-permute-start | bytes 1572872 | tf_op jit(solution)/shard_map/ppermute | solution.py:220
  28.8 28.0 %copy-start.4 = (f32[16,16]{1,0:T(8,128)S(1)}, f32[16,16]{1,0:T(8,128)}, u32[]{:S(2)}) copy-start(f32[16,16]{1,0:T(8,128)} %param.10) | copy-start | bytes 3076
  49.6 24.6 %collective-permute-start.5 = (f32[16,80,64]{1,2,0:T(8,128)}, f32[16,80,64]{1,2,0:T(8,128)}, u32[]{:S(2)}, u32[]{:S(2)}) collective-permute-start(f32[16,80,64]{1,2,0:T(8,128)} %copy.43), channel_id=1, source_target_pairs={{1,0},{2,1},{3,2},{4,3},{5,4},{6,5},{7,6},{0,7},{9,8},{10,9},{11,1... | collective-permute-start | bytes 983048 | tf_op jit(solution)/shard_map/ppermute | solution.py:279
  54.6 20.8 %collective-permute-start.4 = (f32[16,80,64]{1,2,0:T(8,128)}, f32[16,80,64]{1,2,0:T(8,128)}, u32[]{:S(2)}, u32[]{:S(2)}) collective-permute-start(f32[16,80,64]{1,2,0:T(8,128)} %copy.41), channel_id=1, source_target_pairs={{0,1},{1,2},{2,3},{3,4},{4,5},{5,6},{6,7},{7,0},{8,9},{9,10},{10,1... | collective-permute-start | bytes 983048 | tf_op jit(solution)/shard_map/ppermute | solution.py:280
  54.7 24.7 %collective-permute-start.1 = (f32[16,8,1024]{2,1,0:T(8,128)}, f32[16,8,1024]{2,1,0:T(8,128)}, u32[]{:S(2)}, u32[]{:S(2)}) collective-permute-start(f32[16,8,1024]{2,1,0:T(8,128)} %get-tuple-element.8), channel_id=1, source_target_pairs={{8,0},{16,8},{24,16},{9,1},{17,9},{25,17},{10,2},{18,10},{26,18},{... | collective-permute-start | bytes 1572872 | tf_op jit(solution)/shard_map/ppermute | solution.py:221
  80.4 2.4 %copy-start.3 = (f32[16,80,1024]{2,1,0:T(8,128)}, f32[16,80,1024]{2,1,0:T(8,128)S(1)}, u32[]{:S(2)}) copy-start(f32[16,80,1024]{2,1,0:T(8,128)S(1)} %constant_dynamic-update-slice_fusion) | copy-start | bytes 15728644
  85.1 23.7 %collective-permute-start.2 = (f32[16,80,64]{1,2,0:T(8,128)}, f32[16,80,64]{1,2,0:T(8,128)S(1)}, u32[]{:S(2)}, u32[]{:S(2)}) collective-permute-start(f32[16,80,64]{1,2,0:T(8,128)} %copy.34), channel_id=1, source_target_pairs={{0,1},{1,2},{2,3},{3,4},{4,5},{5,6},{6,7},{7,0},{8,9},{9,10},{10,1... | collective-permute-start | bytes 983048 | tf_op jit(solution)/shard_map/ppermute | solution.py:245
  86.3 24.3 %collective-permute-start.3 = (f32[16,80,64]{1,2,0:T(8,128)}, f32[16,80,64]{1,2,0:T(8,128)}, u32[]{:S(2)}, u32[]{:S(2)}) collective-permute-start(f32[16,80,64]{1,2,0:T(8,128)} %copy.35), channel_id=1, source_target_pairs={{1,0},{2,1},{3,2},{4,3},{5,4},{6,5},{7,6},{0,7},{9,8},{10,9},{11,1... | collective-permute-start | bytes 983048 | tf_op jit(solution)/shard_map/ppermute | solution.py:246
  94.0 2.3 %copy-start.2 = (f32[16,80,1024]{2,1,0:T(8,128)}, f32[16,80,1024]{2,1,0:T(8,128)S(1)}, u32[]{:S(2)}) copy-start(f32[16,80,1024]{2,1,0:T(8,128)S(1)} %fusion) | copy-start | bytes 15728644
  97.4 37.6 %collective-permute-start.6 = (f32[16,8,1024]{2,1,0:T(8,128)}, f32[16,8,1024]{2,1,0:T(8,128)S(1)}, u32[]{:S(2)}, u32[]{:S(2)}) collective-permute-start(f32[16,8,1024]{2,1,0:T(8,128)} %get-tuple-element.4), channel_id=1, source_target_pairs={{0,8},{8,16},{16,24},{1,9},{9,17},{17,25},{2,10},{10,18},{18,26},{... | collective-permute-start | bytes 1572872 | tf_op jit(solution)/shard_map/ppermute | solution.py:312
  99.7 35.3 %collective-permute-start.7 = (f32[16,8,1024]{2,1,0:T(8,128)}, f32[16,8,1024]{2,1,0:T(8,128)}, u32[]{:S(2)}, u32[]{:S(2)}) collective-permute-start(f32[16,8,1024]{2,1,0:T(8,128)} %get-tuple-element.5), channel_id=1, source_target_pairs={{8,0},{16,8},{24,16},{9,1},{17,9},{25,17},{10,2},{18,10},{26,18},{... | collective-permute-start | bytes 1572872 | tf_op jit(solution)/shard_map/ppermute | solution.py:311
  112.0 23.0 %slice-start = ((s8[5242880]{0:T(1024)(128)(4,1)}), s8[1048576]{0:T(1024)(128)(4,1)S(1)}, s32[]{:S(2)}) async-start(s8[5242880]{0:T(1024)(128)(4,1)} %bitcast.24), calls=%async_computation.1 | async-start | bytes 2097152
  120.2 2.2 %copy-start.1 = (f32[16,64,1024]{2,1,0:T(8,128)S(1)}, f32[16,64,1024]{2,1,0:T(8,128)}, u32[]{:S(2)}) copy-start(f32[16,64,1024]{2,1,0:T(8,128)} %sigma_ref.3) | copy-start | bytes 12582916
  122.4 12.6 %slice-start.1 = ((s8[5242880]{0:T(1024)(128)(4,1)}), s8[4194304]{0:T(1024)(128)(4,1)S(1)}, s32[]{:S(2)}) async-start(s8[5242880]{0:T(1024)(128)(4,1)} %bitcast.24), calls=%async_computation.2 | async-start | bytes 8388608
where the time goes:
time: 141 us; the launch traced here: 139 us
  local copies, waits for them, and re-layouts  49.8 us (35%)
  Pallas kernels  31.5 us (22%)
  starting transfers between devices  25.7 us (18%)
  waiting for transfers between devices  19 us (13%)
  other arithmetic  11.7 us (8%)
    pallas_call x1, Pallas kernels, local(): pl.pallas_call(adjoint_kernel, grid=(groups + 1,), in_specs=[smem, vmem,...  18.3 us
    pallas_call x1, Pallas kernels, local(): pl.pallas_call(forward_kernel, grid=(groups,), in_specs=[smem, pl.BlockSp...  12.5 us
    unnamed x18, local copies, waits for them, and re-layouts  10.7 us
    ppermute x1, waiting for transfers between devices, local(): to_left = lax.ppermute(ext[:, :, :MAXREACH], 'lon', lon_bwd)  10.3 us
    concatenate x1, local copies, waits for them, and re-layouts, local(): padded = jnp.concatenate([left, tall, right], axis=2)  8.24 us
    mul x4, local copies, waits for them, and re-layouts, kron_matrices(): band.transpose(1, 0, 2)[:, None, :, :, None]  7.13 us
    all_to_all x1, starting transfers between devices, local(): lax.all_to_all(sent, ('lat', 'lon'), split_axis=0, concat_axis=0, tiled=T...  7.1 us
    ppermute x1, waiting for transfers between devices, local(): left = lax.ppermute(tall[:, :, cols - MAXREACH:], 'lon', lon_fwd)  7.08 us
  transfers between devices with their start and end apart: 9, of which 3 were waited for; matrix products, arithmetic and copies ran while one was open for 31% of the time, Pallas kernels for 22%

commit v1 on v0

v1 whole, which is shorter than its diff:
```python
import functools
import math

import jax
import jax.numpy as jnp
from jax import lax
from jax.experimental import pallas as pl
from jax.experimental.pallas import tpu as pltpu
from jax.sharding import PartitionSpec as P

CAP = 64
MAXREACH = 64
MREACH = 8
GROUP = 16
TILE = 128
BF = jnp.bfloat16
F32 = jnp.float32
LOG2E = math.log2(math.e)


def merid_weights(lag):
    taps = [math.exp(-0.5 * (3.0 * t / MREACH) ** 2) for t in range(-MREACH, MREACH + 1)]
    norm = math.sqrt(sum(w * w for w in taps))
    scaled = lag * (3.0 / MREACH)
    return jnp.where(jnp.abs(lag) <= MREACH, jnp.exp(-0.5 * scaled * scaled) / norm, 0.0)


def row_params(zonal_reach):
    reach = zonal_reach.astype(F32)
    t = jnp.arange(-MAXREACH, MAXREACH + 1).astype(F32)
    scaled = 3.0 * t[None, :] / reach[:, None]
    taps = jnp.where(jnp.abs(t)[None, :] <= reach[:, None], jnp.exp(-0.5 * scaled * scaled), 0.0)
    log_norm = -0.5 * jnp.log2(jnp.sum(taps * taps, axis=1))
    return jnp.stack([-4.5 * LOG2E / (reach * reach), log_norm, reach * reach])


def split(x):
    hi = x.astype(BF)
    return hi, (x - hi.astype(F32)).astype(BF)


def dot(a, b):
    return jnp.dot(a, b, preferred_element_type=F32)


def lag_squared():
    p = lax.broadcasted_iota(jnp.int32, (2 * TILE, TILE), 0)
    j = lax.broadcasted_iota(jnp.int32, (2 * TILE, TILE), 1)
    lag = (p - j - MAXREACH).astype(F32)
    return lag * lag


def zonal_rows(hi_ref, lo_ref, out_ref, params_ref, first_row, blocks):
    t2 = lag_squared()
    channels = hi_ref.shape[0] // GROUP
    for r in range(GROUP):
        row = first_row + r
        coef, shift, limit = params_ref[0, row], params_ref[1, row], params_ref[2, row]
        band = jnp.where(t2 <= limit, jnp.exp2(t2 * coef + shift), 0.0)
        band = jnp.concatenate(split(band), axis=1)
        rows = slice(r * channels, (r + 1) * channels)
        parts = []
        for ref in (hi_ref, lo_ref):
            for b in range(blocks):
                parts.append(ref[rows, b * TILE:(b + 2) * TILE])
        prod = dot(jnp.concatenate(parts, axis=0), band)
        n = blocks * channels
        total = prod[:n, :TILE] + (prod[:n, TILE:] + prod[n:, :TILE])
        for b in range(blocks):
            out_ref[rows, b * TILE:(b + 1) * TILE] = total[b * channels:(b + 1) * channels]


MESH = pl.DeviceIdType.MESH


def build_kron(mixing_ref, fwd_hi, fwd_lo, adj_hi, adj_lo):
    channels = mixing_ref.shape[0]
    size = channels * GROUP

    def grid(dim, of):
        index = lax.broadcasted_iota(jnp.int32, (size, size), dim)
        return index % of, index // of

    def spread(matrix, row_fast, col_fast):
        rest = matrix
        rows = lax.broadcasted_iota(jnp.int32, (size, channels), 0)
        rows = rows % channels if row_fast else rows // GROUP
        cols = lax.broadcasted_iota(jnp.int32, (channels, size), 1)
        cols = cols % channels if col_fast else cols // GROUP
        pick_rows = rows == lax.broadcasted_iota(jnp.int32, (size, channels), 1)
        pick_cols = cols == lax.broadcasted_iota(jnp.int32, (channels, size), 0)
        pick_rows = jnp.where(pick_rows, 1.0, 0.0).astype(BF)
        pick_cols = jnp.where(pick_cols, 1.0, 0.0).astype(BF)
        total = jnp.zeros((size, size), F32)
        for _ in range(3):
            part = rest.astype(BF)
            rest = rest - part.astype(F32)
            total = total + dot(dot(pick_rows, part).astype(BF), pick_cols)
        return total

    mixing = mixing_ref[...]
    for hi_ref, lo_ref, mix, a, p in (
        (fwd_hi, fwd_lo, spread(mixing, True, False), grid(0, channels)[1], grid(1, GROUP)[0]),
        (adj_hi, adj_lo, spread(mixing.T, False, True), grid(0, GROUP)[0], grid(1, channels)[1]),
    ):
        for half in range(2):
            hi, lo = split(merid_weights((p - a + (half * GROUP - MREACH)).astype(F32)) * mix)
            hi_ref[half] = hi
            lo_ref[half] = lo


def route_kernel(
    n_lat, n_lon, cols, owner_ref, cell_ref, chan_ref, weight_ref, out_ref,
    sent, got, send_sem, recv_sem,
):
    devices = n_lat * n_lon
    me = lax.axis_index("lat") * n_lon + lax.axis_index("lon")

    def device(k):
        peer = lax.rem(me + k, devices)
        return peer // n_lon, lax.rem(peer, n_lon)

    barrier = pltpu.get_barrier_semaphore()

    def greet(k, _):
        pl.semaphore_signal(barrier, inc=1, device_id=device(k), device_id_type=MESH)
        return 0

    lax.fori_loop(1, devices, greet, 0)
    count = owner_ref.shape[1]
    chunk = math.gcd(count, 256)
    hits = lax.broadcasted_iota(jnp.int32, (devices, count), 0) == owner_ref[...]
    hits_f = jnp.where(hits, 1.0, 0.0)
    hits_b = hits_f.astype(BF)
    upper = (
        lax.broadcasted_iota(jnp.int32, (chunk, chunk), 0)
        < lax.broadcasted_iota(jnp.int32, (chunk, chunk), 1)
    )
    upper = jnp.where(upper, 1.0, 0.0).astype(BF)
    base = jnp.zeros((devices, 1), F32)
    ranks = []
    for k in range(count // chunk):
        part = slice(k * chunk, (k + 1) * chunk)
        before = dot(hits_b[:, part], upper) + base
        ranks.append(jnp.sum(before * hits_f[:, part], axis=0, keepdims=True))
        base = base + jnp.sum(hits_f[:, part], axis=1, keepdims=True)
    rank = jnp.concatenate(ranks, axis=1).astype(jnp.int32)
    rank_hits = lax.broadcasted_iota(jnp.int32, (CAP, count), 0) == rank
    flat = cell_ref[...] + chan_ref[...]
    digits = [flat & 127, (flat >> 7) & 127, flat >> 14]
    pieces = [weight_ref[...].astype(F32)] + [d.astype(F32) for d in digits]
    table = jnp.concatenate([jnp.where(rank_hits, v, 0.0) for v in pieces], axis=0).astype(BF)
    out = lax.dot_general(hits_b, table, (((1,), (1,)), ((), ())), preferred_element_type=F32)
    place = (
        out[:, CAP:2 * CAP] + 128.0 * out[:, 2 * CAP:3 * CAP] + 16384.0 * out[:, 3 * CAP:]
    )
    packed = jnp.concatenate([out[:, :CAP], place], axis=1)
    for d in range(devices):
        sent[d] = packed[d:d + 1]
    pl.semaphore_wait(barrier, devices - 1)

    def copy(k):
        return pltpu.make_async_remote_copy(
            src_ref=sent.at[lax.rem(me + k, devices)],
            dst_ref=got.at[k],
            send_sem=send_sem.at[k],
            recv_sem=recv_sem.at[k],
            device_id=device(k),
            device_id_type=MESH,
        )

    def start(k, _):
        copy(k).start()
        return 0

    def finish(k, _):
        copy(k).wait()
        return 0

    lax.fori_loop(1, devices, start, 0)
    got[0] = sent[me]
    lax.fori_loop(1, devices, finish, 0)
    for k in range(devices // 2):
        first, second = got[2 * k], got[2 * k + 1]
        lanes = slice(2 * CAP * k, 2 * CAP * (k + 1))
        out_ref[0:1, lanes] = jnp.concatenate([first[:, :CAP], second[:, :CAP]], axis=1)
        out_ref[1:2, lanes] = jnp.concatenate([first[:, CAP:], second[:, CAP:]], axis=1)


DIRS = ((-1, 0), (1, 0), (0, -1), (0, 1), (-1, -1), (-1, 1), (1, -1), (1, 1))


def main_kernel(
    n_lat, n_lon, params_ref, got_ref, mixing_ref, control_ref, sigma_ref, inc_ref, grad_ref,
    tall, sigma, inc, grad, ext, colhot, hi_ref, lo_ref, zon_ref, fhi_ref, flo_ref, fzon_ref, carry,
    kron_fh, kron_fl, kron_ah, kron_al,
    rows_in, halo_out, halo_in, edge_in, side_out, side_in, corner_out, corner_in,
    load_sem, store_sem, fsend, frecv, asend, arecv,
):
    channels, rows, cols = control_ref.shape
    received = got_ref.shape[1]
    lines = channels * GROUP
    wide = cols + TILE
    tall_rows = rows + 2 * MREACH
    groups = rows // GROUP
    chunk = math.gcd(received, 2048)
    half_tall, half_rows = tall_rows // 2, rows // 2
    lat, lon = lax.axis_index("lat"), lax.axis_index("lon")

    def there(dlat, dlon):
        return lat + dlat, lax.rem(lon + dlon + n_lon, n_lon)

    def has(dlat):
        return (lat + dlat >= 0) & (lat + dlat < n_lat)

    def when(dlat, action):
        if dlat == 0:
            action()
        else:
            pl.when(has(dlat))(action)

    barrier = pltpu.get_barrier_semaphore()
    for dlat, dlon in DIRS:
        when(dlat, lambda dlat=dlat, dlon=dlon: pl.semaphore_signal(
            barrier, inc=1, device_id=there(dlat, dlon), device_id_type=MESH))
    load_control = pltpu.make_async_copy(
        control_ref, tall.at[:, pl.ds(MREACH, rows), :], load_sem.at[0])
    load_sigma = pltpu.make_async_copy(sigma_ref, sigma, load_sem.at[1])
    load_control.start()
    load_sigma.start()
    sides = jnp.where(lat > 0, 1, 0) + jnp.where(lat < n_lat - 1, 1, 0)
    pl.semaphore_wait(barrier, 2 + 3 * sides)

    def remote(src, dst, sems, index, dlat, dlon):
        return pltpu.make_async_remote_copy(
            src_ref=src, dst_ref=dst, send_sem=sems[0].at[index], recv_sem=sems[1].at[index],
            device_id=there(dlat, dlon), device_id_type=MESH)

    row_copies = [
        remote(control_ref.at[:, pl.ds(0, MREACH), :], rows_in.at[0], (fsend, frecv), 0, -1, 0),
        remote(control_ref.at[:, pl.ds(rows - MREACH, MREACH), :], rows_in.at[1],
               (fsend, frecv), 1, 1, 0),
    ]
    halo_copies = [
        remote(halo_out.at[0], halo_in.at[0], (fsend, frecv), 2, 0, -1),
        remote(halo_out.at[1], halo_in.at[1], (fsend, frecv), 3, 0, 1),
    ]
    when(-1, row_copies[0].start)
    when(1, row_copies[1].start)

    def place(k):
        flat = got_ref[1:2, pl.ds(k * chunk, chunk)].astype(jnp.int32)
        return got_ref[0:1, pl.ds(k * chunk, chunk)], flat

    build_kron(mixing_ref, kron_fh, kron_fl, kron_ah, kron_al)
    carry[...] = jnp.zeros_like(carry)
    hi_ref[...] = jnp.zeros_like(hi_ref)
    lo_ref[...] = jnp.zeros_like(lo_ref)
    for k in range(received // chunk):
        col = place(k)[1] % cols
        hot = lax.broadcasted_iota(jnp.int32, (cols, chunk), 0) == col
        colhot[:, k * chunk:(k + 1) * chunk] = jnp.where(hot, 1.0, 0.0).astype(BF)
    load_sigma.wait()

    def send_halo():
        load_control.wait()
        for index, dlat, start in ((0, -1, rows + MREACH), (1, 1, 0)):
            when(dlat, row_copies[index].wait_send)

            @pl.when(has(-dlat))
            def _():
                row_copies[index].wait_recv()
                tall[:, start:start + MREACH, :] = rows_in[index]

            @pl.when(jnp.logical_not(has(-dlat)))
            def _():
                tall[:, start:start + MREACH, :] = jnp.zeros((channels, MREACH, cols), F32)
        for index, lanes in ((0, slice(0, MAXREACH)), (1, slice(TILE - MAXREACH, TILE))):
            tile = slice(0, TILE) if index == 0 else slice(cols - TILE, cols)
            top = tall[:, :half_tall, tile][:, :, lanes]
            bottom = tall[:, half_tall:, tile][:, :, lanes]
            halo_out[index] = jnp.concatenate([top, bottom], axis=2)
        for copy in halo_copies:
            copy.start()

    def adjoint_group(g, _):
        pl.when(g == 1)(send_halo)
        place_ids = lax.broadcasted_iota(jnp.int32, (lines, chunk), 0)
        total = jnp.zeros((lines, cols), F32)
        for k in range(received // chunk):
            value, flat = place(k)
            line = flat // cols
            chan, row = line // rows, line % rows - g * GROUP
            inside = (row >= 0) & (row < GROUP)
            target = jnp.where(inside, chan * GROUP + row, -1)
            rowhot = jnp.where(place_ids == target, value, 0.0).astype(BF)
            total = total + lax.dot_general(
                rowhot, colhot[:, k * chunk:(k + 1) * chunk],
                (((1,), (1,)), ((), ())), preferred_element_type=F32,
            )
        here = pl.ds(pl.multiple_of(g * GROUP, GROUP), GROUP)
        weighted = total.reshape(channels, GROUP, cols) * sigma[:, here, :]
        hi, lo = split(jnp.swapaxes(weighted, 0, 1).reshape(lines, cols))
        hi_ref[:, TILE:TILE + cols] = hi
        lo_ref[:, TILE:TILE + cols] = lo
        zonal_rows(hi_ref, lo_ref, zon_ref, params_ref, g * GROUP, wide // TILE)
        z_hi, z_lo = split(zon_ref[...])
        done = carry[...] + (
            dot(kron_ah[1], z_hi) + (dot(kron_ah[1], z_lo) + dot(kron_al[1], z_hi))
        )
        ext[:, here, :] = done.reshape(channels, GROUP, wide)
        carry[...] = dot(kron_ah[0], z_hi) + (dot(kron_ah[0], z_lo) + dot(kron_al[0], z_hi))
        return 0

    lax.fori_loop(0, groups, adjoint_group, 0)
    ext[:, rows:rows + GROUP, :] = carry[...].reshape(channels, GROUP, wide)

    for index, tile in ((0, slice(0, TILE)), (1, slice(wide - TILE, wide))):
        lanes = slice(0, MAXREACH) if index == 0 else slice(TILE - MAXREACH, TILE)
        top = ext[:, MREACH:MREACH + half_rows, tile][:, :, lanes]
        bottom = ext[:, MREACH + half_rows:MREACH + rows, tile][:, :, lanes]
        side_out[index] = jnp.concatenate([top, bottom], axis=2)
        corner_out[index] = ext[:, :MREACH, tile]
        corner_out[2 + index] = ext[:, rows + MREACH:, tile]
    sems = (asend, arecv)
    fringe = [
        remote(ext.at[:, pl.ds(0, MREACH), :], edge_in.at[0], sems, 0, -1, 0),
        remote(ext.at[:, pl.ds(rows + MREACH, MREACH), :], edge_in.at[1], sems, 1, 1, 0),
        remote(side_out.at[0], side_in.at[0], sems, 2, 0, -1),
        remote(side_out.at[1], side_in.at[1], sems, 3, 0, 1),
    ] + [
        remote(corner_out.at[i], corner_in.at[i], sems, 4 + i, *DIRS[4 + i]) for i in range(4)
    ]
    for (dlat, _), copy in zip(DIRS, fringe):
        when(dlat, copy.start)

    for copy in halo_copies:
        copy.wait()

    def forward_group(e, _):
        here = pl.ds(pl.multiple_of(e * GROUP, GROUP), GROUP)
        body = tall[:, here, :]

        def column(packed_ref):
            pieces = []
            for part in range(GROUP // 8):
                first = e * GROUP + part * 8
                second = first >= half_tall
                line = pl.multiple_of(jnp.where(second, first - half_tall, first), 8)
                both = packed_ref[:, pl.ds(line, 8), :]
                pieces.append(jnp.where(second, both[:, :, MAXREACH:], both[:, :, :MAXREACH]))
            return jnp.concatenate(pieces, axis=1)

        block = jnp.concatenate([column(halo_in.at[1]), body, column(halo_in.at[0])], axis=2)
        e_hi, e_lo = split(block.reshape(lines, wide))

        @pl.when(e > 0)
        def _():
            total = carry[...] + (
                dot(kron_fh[1], e_hi) + (dot(kron_fh[1], e_lo) + dot(kron_fl[1], e_hi))
            )
            hi, lo = split(total)
            fhi_ref[...] = hi
            flo_ref[...] = lo
            first = (e - 1) * GROUP
            zonal_rows(fhi_ref, flo_ref, fzon_ref, params_ref, first, cols // TILE)
            smooth = jnp.swapaxes(fzon_ref[...].reshape(GROUP, channels, cols), 0, 1)
            there_rows = pl.ds(pl.multiple_of(first, GROUP), GROUP)
            inc[:, there_rows, :] = smooth * sigma[:, there_rows, :]
        carry[...] = dot(kron_fh[0], e_hi) + (dot(kron_fh[0], e_lo) + dot(kron_fl[0], e_hi))
        return 0

    lax.fori_loop(0, groups + 1, forward_group, 0)
    store_inc = pltpu.make_async_copy(inc, inc_ref, store_sem.at[0])
    store_inc.start()

    grad[...] = ext[:, MREACH:MREACH + rows, MAXREACH:MAXREACH + cols]
    first_tile, last_tile = slice(0, TILE), slice(cols - TILE, cols)
    for (dlat, _), copy in zip(DIRS, fringe):
        when(dlat, copy.wait_send)
        when(-dlat, copy.wait_recv)
    zero = jnp.zeros((channels, half_rows, MAXREACH), F32)
    for part in range(2):
        lanes = slice(part * MAXREACH, (part + 1) * MAXREACH)
        span = slice(part * half_rows, (part + 1) * half_rows)
        grad[:, span, last_tile] += jnp.concatenate([zero, side_in[0][:, :, lanes]], axis=2)
        grad[:, span, first_tile] += jnp.concatenate([side_in[1][:, :, lanes], zero], axis=2)
    small = jnp.zeros((channels, MREACH, MAXREACH), F32)
    for index, dlat, span in ((0, -1, slice(rows - MREACH, rows)), (1, 1, slice(0, MREACH))):
        @pl.when(has(-dlat))
        def _():
            grad[:, span, :] += edge_in[index][:, :, MAXREACH:MAXREACH + cols]
            right, left = corner_in[2 * index], corner_in[2 * index + 1]
            grad[:, span, last_tile] += jnp.concatenate([small, right[:, :, :MAXREACH]], axis=2)
            grad[:, span, first_tile] += jnp.concatenate([left[:, :, MAXREACH:], small], axis=2)
    store_grad = pltpu.make_async_copy(grad, grad_ref, store_sem.at[1])
    store_grad.start()
    store_inc.wait()
    store_grad.wait()


def local(
    n_lat, n_lon, control, sigma_field, mixing, zonal_reach, obs_owner, obs_cell, obs_chan, obs_weight
):
    channels, rows, cols = control.shape
    devices = n_lat * n_lon
    received = devices * CAP
    lines, wide = channels * GROUP, cols + TILE
    count = obs_cell.shape[0]
    smem = pl.BlockSpec(memory_space=pltpu.SMEM)
    vmem = pl.BlockSpec(memory_space=pltpu.VMEM)
    anywhere = pl.BlockSpec(memory_space=pl.ANY)
    got = pl.pallas_call(
        lambda *refs: route_kernel(n_lat, n_lon, cols, *refs),
        out_shape=jax.ShapeDtypeStruct((2, received), F32),
        in_specs=[vmem] * 4,
        out_specs=vmem,
        scratch_shapes=[
            pltpu.VMEM((devices, 1, 2 * CAP), F32),
            pltpu.VMEM((devices, 1, 2 * CAP), F32),
            pltpu.SemaphoreType.DMA((devices,)),
            pltpu.SemaphoreType.DMA((devices,)),
        ],
        compiler_params=pltpu.CompilerParams(
            vmem_limit_bytes=32 * 2**20, collective_id=0, has_side_effects=True
        ),
        name="route",
    )(
        obs_owner.reshape(1, count),
        obs_cell.reshape(1, count),
        (obs_chan * (rows * cols)).reshape(1, count),
        obs_weight.reshape(1, count),
    )
    tall_rows = rows + 2 * MREACH
    halo = pltpu.VMEM((2, channels, tall_rows // 2, TILE), F32)
    side = pltpu.VMEM((2, channels, rows // 2, TILE), F32)
    corner = pltpu.VMEM((4, channels, MREACH, TILE), F32)
    kron = pltpu.VMEM((2, lines, lines), BF)
    out = jax.ShapeDtypeStruct((channels, rows, cols), F32)
    return pl.pallas_call(
        lambda *refs: main_kernel(n_lat, n_lon, *refs),
        out_shape=(out, out),
        in_specs=[smem, vmem, vmem, anywhere, anywhere],
        out_specs=(anywhere, anywhere),
        scratch_shapes=[
            pltpu.VMEM((channels, tall_rows, cols), F32),
            pltpu.VMEM((channels, rows, cols), F32),
            pltpu.VMEM((channels, rows, cols), F32),
            pltpu.VMEM((channels, rows, cols), F32),
            pltpu.VMEM((channels, tall_rows, wide), F32),
            pltpu.VMEM((cols, received), BF),
            pltpu.VMEM((lines, wide + TILE), BF),
            pltpu.VMEM((lines, wide + TILE), BF),
            pltpu.VMEM((lines, wide), F32),
            pltpu.VMEM((lines, wide), BF),
            pltpu.VMEM((lines, wide), BF),
            pltpu.VMEM((lines, cols), F32),
            pltpu.VMEM((lines, wide), F32),
            kron, kron, kron, kron,
            pltpu.VMEM((2, channels, MREACH, cols), F32),
            halo, halo,
            pltpu.VMEM((2, channels, MREACH, wide), F32),
            side, side, corner, corner,
            pltpu.SemaphoreType.DMA((2,)),
            pltpu.SemaphoreType.DMA((2,)),
            pltpu.SemaphoreType.DMA((4,)),
            pltpu.SemaphoreType.DMA((4,)),
            pltpu.SemaphoreType.DMA((8,)),
            pltpu.SemaphoreType.DMA((8,)),
        ],
        compiler_params=pltpu.CompilerParams(
            vmem_limit_bytes=60 * 2**20, collective_id=1, has_side_effects=True
        ),
        name="main",
    )(row_params(zonal_reach), got, mixing, control, sigma_field)


def solution(mesh):
    return jax.shard_map(
        functools.partial(local, mesh.shape["lat"], mesh.shape["lon"]),
        mesh=mesh,
        in_specs=(
            P(None, "lat", "lon"),
            P(None, "lat", "lon"),
            P(),
            P("lat"),
            P(("lat", "lon"), None),
            P(("lat", "lon")),
            P(("lat", "lon")),
            P(("lat", "lon")),
        ),
        out_specs=(P(None, "lat", "lon"), P(None, "lat", "lon")),
        check_vma=False,
    )
```

time: 141 us -> 76.6 us (0.54); the launches traced: 139 us -> 76.1 us
  local copies, waits for them, and re-layouts: 49.8 us -> 9.64 us
  Pallas kernels: 31.5 us -> 63 us
  starting transfers between devices: 25.7 us -> 0 us
  waiting for transfers between devices: 19 us -> 0 us
  other arithmetic: 11.7 us -> 2.83 us
    pallas_call x3 -> x2, Pallas kernels: 31.5 us -> 63 us  [the longest x1 53 us: local(): pl.pallas_call(lambda *refs: main_kernel(n_lat, n_lon, *refs), out_shape=...]
    ppermute x8 -> x0, waiting for transfers between devices: 19 us -> none  [the longest x1 10.3 us: local(): to_left = lax.ppermute(ext[:, :, :MAXREACH], 'lon', lon_bwd)]
    ppermute x8 -> x0, starting transfers between devices: 18.6 us -> none  [the longest x1 3.98 us: local(): to_left = lax.ppermute(ext[:, :, :MAXREACH], 'lon', lon_bwd)]
    mul x8 -> x0, local copies, waits for them, and re-layouts: 14.2 us -> none  [the longest x4 7.13 us: kron_matrices(): band.transpose(1, 0, 2)[:, None, :, :, None]]
    concatenate x2 -> x0, local copies, waits for them, and re-layouts: 9.32 us -> none  [the longest x1 8.24 us: local(): padded = jnp.concatenate([left, tall, right], axis=2)]
    slice x8 -> x0, local copies, waits for them, and re-layouts: 9.25 us -> none  [the longest x2 2.6 us: local(): to_right = lax.ppermute(ext[:, :, cols + MAXREACH:], 'lon', lon_fwd)]
    add x3 -> x0, other arithmetic: 8.63 us -> none  [the longest x1 4.3 us: local(): inner = inner + jnp.pad(to_left, ((0, 0), (0, 0), (cols - MAXREACH, 0)))]
    all_to_all x1 -> x0, starting transfers between devices: 7.1 us -> none  [local(): lax.all_to_all(sent, ('lat', 'lon'), split_axis=0, concat_axis=0, tiled=T...]
  transfers between devices with their start and end apart: 9 -> 0, of which waited for: 3 -> 0; matrix products, arithmetic and copies ran while one was open for 31% -> 0% of each run, Pallas kernels for 22% -> 0%
where the time goes in v1:
time: 76.6 us; the launch traced here: 76.1 us
  Pallas kernels  63 us (82%)
  local copies, waits for them, and re-layouts  9.64 us (13%)
  other arithmetic  2.83 us (4%)
    pallas_call x1, Pallas kernels, local(): pl.pallas_call(lambda *refs: main_kernel(n_lat, n_lon, *refs), out_shape=...  53 us
    pallas_call x1, Pallas kernels, local(): pl.pallas_call(lambda *refs: route_kernel(n_lat, n_lon, cols, *refs), out...  9.98 us
    unnamed x10, local copies, waits for them, and re-layouts  8.95 us

profile of v1, /device:TPU:1, one launch (start us, length us, event | category | flops | bytes accessed | tf_op | source)
XLA Modules:
  0.0 76.1 jit_solution(6283273929934125289)
XLA Ops:
  0.6 0.7 convert_element_type.15
  1.3 0.7 divide_bitcast_fusion
  2.0 0.2 fusion.3
  2.2 0.6 pad_maximum_fusion.refs_0_
  2.8 0.7 broadcast_multiply_fusion
  3.5 0.7 reshape.43.refs_3_
  4.2 0.0 copy-start.1
  4.2 0.7 copy-done.1
  4.9 0.0 copy-start.2
  4.9 0.7 copy-done.2
  5.6 10.0 %route.1.refs_1_ = f32[2,2048]{1,0:T(2,128)S(1)} custom-call(s32[1,2048]{1,0:T(1,128)S(1)} %bitcast.10, s32[1,2048]{1,0:T(1,128)S(1)} %bitcast.11, s32[1,2048]{1,0:T(1,128)S(1)} %bitcast.9, bf16[1,2048]{1,0:T(2,128)(2,1)S(1)} %reshape.43.refs_3_), custom_call_target="tpu_custom_call" | custom-call | tf_op jit(solution)/shard_map/route/pallas_call | solution.py:413
  15.5 0.0 copy-start
  15.6 0.6 copy-done
  16.2 53.0 %main.1 = (f32[16,64,1024]{2,1,0:T(8,128)}, f32[16,64,1024]{2,1,0:T(8,128)}) custom-call(f32[3,64]{1,0:T(4,128)} %pad_maximum_fusion.refs_0_, f32[2,2048]{1,0:T(2,128)} %copy-done, f32[16,16]{1,0:T(8,128)} %refs_2_.1, f32[16,64,1024]{2,1,0:T(8,128)} %refs_3_.1, f32[16,64,1024]{2,1,0:T(8,128)} %refs_4_.1), custom_call_target="tpu_custom_call" | custom-call | tf_op jit(solution)/shard_map/main/pallas_call | solution.py:440
  69.2 0.0 copy-start.3
  69.2 4.9 %copy.12 = f32[16,64,1024]{2,1,0:T(8,128)} copy(f32[16,64,1024]{2,1,0:T(8,128)} %get-tuple-element.8) | data formatting | bytes 8388608
  74.1 0.0 copy-done.3
  74.1 2.0 %copy.13 = f32[16,64,1024]{2,1,0:T(8,128)} copy(f32[16,64,1024]{2,1,0:T(8,128)S(1)} %copy-done.3) | data formatting | bytes 8388608
  (2 shorter events, 0.0 us)
Async XLA Ops:
  4.2 0.7 copy-start.1
  4.9 0.7 copy-start.2
  15.5 0.6 copy-start
  69.2 5.0 %copy-start.3 = (f32[16,64,1024]{2,1,0:T(8,128)S(1)}, f32[16,64,1024]{2,1,0:T(8,128)}, u32[]{:S(2)}) copy-start(f32[16,64,1024]{2,1,0:T(8,128)} %get-tuple-element.9) | copy-start | bytes 12582916

commit v2 on v1

--- a/solution.py
+++ b/solution.py
@@ -25,15 +25,6 @@
     return jnp.where(jnp.abs(lag) <= MREACH, jnp.exp(-0.5 * scaled * scaled) / norm, 0.0)
 
 
-def row_params(zonal_reach):
-    reach = zonal_reach.astype(F32)
-    t = jnp.arange(-MAXREACH, MAXREACH + 1).astype(F32)
-    scaled = 3.0 * t[None, :] / reach[:, None]
-    taps = jnp.where(jnp.abs(t)[None, :] <= reach[:, None], jnp.exp(-0.5 * scaled * scaled), 0.0)
-    log_norm = -0.5 * jnp.log2(jnp.sum(taps * taps, axis=1))
-    return jnp.stack([-4.5 * LOG2E / (reach * reach), log_norm, reach * reach])
-
-
 def split(x):
     hi = x.astype(BF)
     return hi, (x - hi.astype(F32)).astype(BF)
@@ -50,12 +41,19 @@
     return lag * lag
 
 
-def zonal_rows(hi_ref, lo_ref, out_ref, params_ref, first_row, blocks):
+def zonal_rows(hi_ref, lo_ref, out_ref, reach_ref, first_row, blocks):
     t2 = lag_squared()
+    side2 = (lax.broadcasted_iota(jnp.int32, (1, TILE), 1) + 1).astype(F32)
+    side2 = side2 * side2
     channels = hi_ref.shape[0] // GROUP
     for r in range(GROUP):
         row = first_row + r
-        coef, shift, limit = params_ref[0, row], params_ref[1, row], params_ref[2, row]
+        reach = reach_ref[row].astype(F32)
+        limit = jnp.full((1, TILE), reach * reach)
+        coef = (-4.5 * LOG2E) / limit
+        side = jnp.where(side2 <= limit, jnp.exp2(side2 * coef), 0.0)
+        norm = 2.0 * jnp.sum(side * side, axis=1, keepdims=True) + 1.0
+        shift = -0.5 * jnp.log2(norm)
         band = jnp.where(t2 <= limit, jnp.exp2(t2 * coef + shift), 0.0)
         band = jnp.concatenate(split(band), axis=1)
         rows = slice(r * channels, (r + 1) * channels)
@@ -191,7 +189,7 @@
 
 
 def main_kernel(
-    n_lat, n_lon, params_ref, got_ref, mixing_ref, control_ref, sigma_ref, inc_ref, grad_ref,
+    n_lat, n_lon, reach_ref, got_ref, mixing_ref, control_ref, sigma_ref, inc_ref, grad_ref,
     tall, sigma, inc, grad, ext, colhot, hi_ref, lo_ref, zon_ref, fhi_ref, flo_ref, fzon_ref, carry,
     kron_fh, kron_fl, kron_ah, kron_al,
     rows_in, halo_out, halo_in, edge_in, side_out, side_in, corner_out, corner_in,
@@ -303,7 +301,7 @@
         hi, lo = split(jnp.swapaxes(weighted, 0, 1).reshape(lines, cols))
         hi_ref[:, TILE:TILE + cols] = hi
         lo_ref[:, TILE:TILE + cols] = lo
-        zonal_rows(hi_ref, lo_ref, zon_ref, params_ref, g * GROUP, wide // TILE)
+        zonal_rows(hi_ref, lo_ref, zon_ref, reach_ref, g * GROUP, wide // TILE)
         z_hi, z_lo = split(zon_ref[...])
         done = carry[...] + (
             dot(kron_ah[1], z_hi) + (dot(kron_ah[1], z_lo) + dot(kron_al[1], z_hi))
@@ -363,7 +361,7 @@
             fhi_ref[...] = hi
             flo_ref[...] = lo
             first = (e - 1) * GROUP
-            zonal_rows(fhi_ref, flo_ref, fzon_ref, params_ref, first, cols // TILE)
+            zonal_rows(fhi_ref, flo_ref, fzon_ref, reach_ref, first, cols // TILE)
             smooth = jnp.swapaxes(fzon_ref[...].reshape(GROUP, channels, cols), 0, 1)
             there_rows = pl.ds(pl.multiple_of(first, GROUP), GROUP)
             inc[:, there_rows, :] = smooth * sigma[:, there_rows, :]
@@ -469,10 +467,10 @@
             pltpu.SemaphoreType.DMA((8,)),
         ],
         compiler_params=pltpu.CompilerParams(
-            vmem_limit_bytes=60 * 2**20, collective_id=1, has_side_effects=True
+            vmem_limit_bytes=42 * 2**20 + 2 * cols * received, collective_id=1, has_side_effects=True
         ),
         name="main",
-    )(row_params(zonal_reach), got, mixing, control, sigma_field)
+    )(zonal_reach, got, mixing, control, sigma_field)
 
 
 def solution(mesh):

time: 76.6 us -> 74.2 us (0.969)
  other arithmetic: 2.83 us -> 0.7 us
    another operation x2 -> x0, other arithmetic: 1.26 us -> none  [row_params(): return jnp.stack([-4.5 * LOG2E / (reach * reach), log_norm, reach * reach])]
    unnamed x10 -> x12, local copies, waits for them, and re-layouts: 8.95 us -> 8.45 us
where the time goes in v2:
time: 74.2 us; the launch traced here: 73.7 us
  Pallas kernels  63.2 us (85%)
  local copies, waits for them, and re-layouts  9.14 us (12%)
    pallas_call x1, Pallas kernels, local(): pl.pallas_call(lambda *refs: main_kernel(n_lat, n_lon, *refs), out_shape=...  53.3 us
    pallas_call x1, Pallas kernels, local(): pl.pallas_call(lambda *refs: route_kernel(n_lat, n_lon, cols, *refs), out...  9.98 us
    unnamed x12, local copies, waits for them, and re-layouts  8.45 us

profile of v2, /device:TPU:1, one launch (start us, length us, event | category | flops | bytes accessed | tf_op | source)
XLA Modules:
  0.0 73.7 jit_solution(6304968782657903300)
XLA Ops:
  0.6 0.7 broadcast_multiply_fusion
  1.3 0.7 reshape.19.refs_3_
  2.0 0.0 copy-start.1
  2.0 0.7 copy-done.1
  2.7 0.0 copy-start.2
  2.7 0.7 copy-done.2
  3.4 10.0 %route.1.refs_1_ = f32[2,2048]{1,0:T(2,128)S(1)} custom-call(s32[1,2048]{1,0:T(1,128)S(1)} %bitcast.4, s32[1,2048]{1,0:T(1,128)S(1)} %bitcast.5, s32[1,2048]{1,0:T(1,128)S(1)} %bitcast.3, bf16[1,2048]{1,0:T(2,128)(2,1)S(1)} %reshape.19.refs_3_), custom_call_target="tpu_custom_call" | custom-call | tf_op jit(solution)/shard_map/route/pallas_call | solution.py:411
  13.4 0.0 copy-start
  13.4 0.7 copy-done
  14.1 0.0 copy-start.3
  14.1 0.7 copy-done.3
  14.8 53.3 %main.1 = (f32[16,64,1024]{2,1,0:T(8,128)S(1)}, f32[16,64,1024]{2,1,0:T(8,128)}) custom-call(s32[64]{0:T(128)S(1)} %copy-done.3, f32[2,2048]{1,0:T(2,128)S(1)} %route.1.refs_1_, f32[16,16]{1,0:T(8,128)S(1)} %copy-done, f32[16,64,1024]{2,1,0:T(8,128)} %refs_3_.1, f32[16,64,1024]{2,1,0:T(8,128)} %refs_4_.1), custom_call_target="tpu_custom_call" | custom-call | tf_op jit(solution)/shard_map/main/pallas_call | solution.py:438
  68.0 0.0 copy-start.4
  68.0 2.1 %copy.12 = f32[16,64,1024]{2,1,0:T(8,128)} copy(f32[16,64,1024]{2,1,0:T(8,128)S(1)} %get-tuple-element.4) | data formatting | bytes 8388608
  70.2 1.6 %copy-done.4 = f32[16,64,1024]{2,1,0:T(8,128)S(1)} copy-done((f32[16,64,1024]{2,1,0:T(8,128)S(1)}, f32[16,64,1024]{2,1,0:T(8,128)}, u32[]{:S(2)}) %copy-start.4) | copy-done | bytes 4194328
  71.7 2.0 %copy.13 = f32[16,64,1024]{2,1,0:T(8,128)} copy(f32[16,64,1024]{2,1,0:T(8,128)S(1)} %copy-done.4) | data formatting | bytes 8388608
Async XLA Ops:
  2.0 0.7 copy-start.1
  2.7 0.7 copy-start.2
  13.4 0.7 copy-start
  14.1 0.7 copy-start.3
  68.0 3.7 %copy-start.4 = (f32[16,64,1024]{2,1,0:T(8,128)S(1)}, f32[16,64,1024]{2,1,0:T(8,128)}, u32[]{:S(2)}) copy-start(f32[16,64,1024]{2,1,0:T(8,128)} %get-tuple-element.5) | copy-start | bytes 12582916
